TPU v7x, 128 devices: a whole 4x4x4 slice. The times are simulated.
128 devices in a mesh: gx: 8 (over z, x_hi), gy: 4 (over x_lo, core), gz: 4 (over y).
Axes of the slice: x: 4 (x_hi: 2, x_lo: 2; x = x_hi * 2 + x_lo), y: 4, z: 4, core: 2. Of those that a mesh axis runs over, the one named last changes fastest.
Arguments:
- layer_input: bfloat16 [4, 1024, 16384], P('gy', 'gz', 'gx'), may hold values from -6 to 6
- qkv_grad: bfloat16 [4, 1024, 9216], P('gy', 'gx', 'gz'), may hold values from -0.25 to 0.25
- qkv_weight: bfloat16 [16384, 9216], P(('gx', 'gy'), 'gz'), may hold values from -6 to 6
Outputs:
- input_grad: bfloat16 [4, 1024, 16384], P('gy', None, ('gx', 'gz'))
- weight_grad: bfloat16 [16384, 9216], P(('gx', 'gy'), 'gz')
All inputs are finite; a program needn't handle non-finite values.
Results may differ from a plain program's by a relative error of at most 0.015.
Values may be sent and summed in bfloat16 or wider, within the bound.
A program may use at most 128 MiB of HBM per device.

v0:
```python
import jax
import jax.numpy as jnp
from jax import lax
from jax.sharding import PartitionSpec as P


def body(layer_input, qkv_grad, qkv_weight):
    grads_all = lax.all_gather(qkv_grad, "gx", axis=1, tiled=True)
    grad_rows = grads_all[0]
    product = lax.dot_general(
        grad_rows,
        lax.all_gather(qkv_weight, "gy", axis=0, tiled=True),
        (((1,), (1,)), ((), ())),
        preferred_element_type=jnp.float32,
    )
    partial_value = product[None]
    input_grad = lax.psum_scatter(
        partial_value.astype(jnp.bfloat16), "gz", scatter_dimension=2, tiled=True
    )
    inputs_all = lax.all_gather(layer_input, "gz", axis=1, tiled=True)
    input_rows = inputs_all[0]
    weight_grad = lax.psum_scatter(
        lax.dot_general(
            input_rows, grad_rows, (((0,), (0,)), ((), ())), preferred_element_type=jnp.float32
        ).astype(jnp.bfloat16),
        "gy",
        scatter_dimension=0,
        tiled=True,
    )
    return (input_grad, weight_grad)


def solution(mesh):
    return jax.shard_map(
        body,
        mesh=mesh,
        in_specs=(P("gy", "gz", "gx"), P("gy", "gx", "gz"), P(("gx", "gy"), "gz")),
        out_specs=(P("gy", None, ("gx", "gz")), P(("gx", "gy"), "gz")),
        check_vma=False,
    )
```

profile of v0, /device:TPU:3, one launch (start us, length us, event | category | flops | bytes accessed | tf_op | source)
XLA Modules:
  0.0 374.9 jit_solution(16986912488004614591)
XLA Ops:
  7.2 0.0 all-gather.4.cloned.1.call-start
  7.2 0.7 all-gather.4.cloned.1.call-update
  7.9 0.0 all-gather.6.cloned.1.call-start
  7.9 0.7 all-gather.6.cloned.1.call-update
  8.6 0.0 all-gather.8.cloned.1.call-start
  8.7 0.7 all-gather.8.cloned.1.call-update
  9.4 0.0 reduce-scatter.3.cloned.1.call-start
  9.4 77.9 %all-gather.4.cloned.1.call-done = bf16[1,1024,2304]{2,1,0:T(8,128)(2,1)} async-done(((bf16[1,128,2304]{2,1,0:T(8,128)(2,1)}), bf16[1,1024,2304]{2,1,0:T(8,128)(2,1)}) %all-gather.4.cloned.1.call-update) | async-done | bytes 4718608 | tf_op jit(solution)/shard_map/all_gather | solution.py:8
  87.3 90.1 %all-gather.6.cloned.1.call-done = bf16[2048,2304]{1,0:T(8,128)(2,1)} async-done(((bf16[512,2304]{1,0:T(8,128)(2,1)}), bf16[2048,2304]{1,0:T(8,128)(2,1)}) %all-gather.6.cloned.1.call-update) | async-done | bytes 9437200 | tf_op jit(solution)/shard_map/all_gather | solution.py:12
  177.5 15.3 %convert_bitcast_fusion = bf16[1,1024,2048]{2,1,0:T(8,128)(2,1)} fusion(bf16[2048,2304]{1,0:T(8,128)(2,1)} %all-gather.6.cloned.1.call-done, bf16[1,1024,2304]{2,1,0:T(8,128)(2,1)} %all-gather.4.cloned.1.call-done), kind=kOutput, calls=%fused_computation.5 | convolution fusion | flops 9665773568 | bytes 18350080 | tf_op jit(solution)/shard_map/dot_general | solution.py:10
  192.8 0.0 reduce-scatter.3.cloned.1.call-update
  192.8 0.0 reduce-scatter.5.cloned.1.call-start
  192.9 36.2 %all-gather.8.cloned.1.call-done = bf16[1,1024,2048]{2,1,0:T(8,128)(2,1)} async-done(((bf16[1,256,2048]{2,1,0:T(8,128)(2,1)}), bf16[1,1024,2048]{2,1,0:T(8,128)(2,1)}) %all-gather.8.cloned.1.call-update) | async-done | bytes 4194320 | tf_op jit(solution)/shard_map/all_gather | solution.py:20
  229.1 15.4 %convolution_convert_fusion = bf16[2048,2304]{1,0:T(8,128)(2,1)} fusion(bf16[1,1024,2304]{2,1,0:T(8,128)(2,1)} %all-gather.4.cloned.1.call-done, bf16[1,1024,2048]{2,1,0:T(8,128)(2,1)} %all-gather.8.cloned.1.call-done), kind=kOutput, calls=%fused_computation | convolution fusion | flops 9668395008 | bytes 18350080 | tf_op jit(solution)/shard_map/dot_general | solution.py:23
  244.5 0.0 reduce-scatter.5.cloned.1.call-update
  244.5 34.6 %reduce-scatter.3.cloned.1.call-done = bf16[1,1024,512]{2,1,0:T(8,128)(2,1)} async-done(((bf16[1,1024,2048]{2,1,0:T(8,128)(2,1)}), bf16[1,1024,512]{2,1,0:T(8,128)(2,1)}) %reduce-scatter.3.cloned.1.call-update) | async-done | bytes 1048592 | tf_op jit(solution)/shard_map/reduce_scatter | solution.py:17
  279.1 89.3 %reduce-scatter.5.cloned.1.call-done = bf16[512,2304]{1,0:T(8,128)(2,1)} async-done(((bf16[2048,2304]{1,0:T(8,128)(2,1)}), bf16[512,2304]{1,0:T(8,128)(2,1)}) %reduce-scatter.5.cloned.1.call-update) | async-done | bytes 2359312 | tf_op jit(solution)/shard_map/reduce_scatter | solution.py:22
Async XLA Ops:
  7.2 80.2 %all-gather.4.cloned.1.call-start = ((), (), s32[]{:S(2)}) async-start(), calls=%async_computation.2 | async-start | bytes 5308416 | tf_op jit(solution)/shard_map/all_gather | solution.py:8
  7.9 169.6 %all-gather.6.cloned.1.call-start = ((), (), s32[]{:S(2)}) async-start(), calls=%async_computation.3 | async-start | bytes 11796480 | tf_op jit(solution)/shard_map/all_gather | solution.py:12
  8.6 220.4 %all-gather.8.cloned.1.call-start = ((), (), s32[]{:S(2)}) async-start(), calls=%async_computation.5 | async-start | bytes 5242880 | tf_op jit(solution)/shard_map/all_gather | solution.py:20
  9.4 269.7 %reduce-scatter.3.cloned.1.call-start = ((), (), s32[]{:S(2)}) async-start(), calls=%async_computation.4 | async-start | bytes 5242880 | tf_op jit(solution)/shard_map/reduce_scatter | solution.py:17
  192.8 175.6 %reduce-scatter.5.cloned.1.call-start = ((), (), s32[]{:S(2)}) async-start(), calls=%async_computation.6 | async-start | bytes 11796480 | tf_op jit(solution)/shard_map/reduce_scatter | solution.py:22
Sparse Core Ops, SparseCore 0:
  10.3 76.9 all-gather.3
  89.0 88.4 all-gather.5
  179.1 49.8 all-gather.7
  231.9 47.1 reduce-scatter.2
  282.1 86.1 reduce-scatter.4
where the time goes:
time: 377 us; the launch traced here: 375 us
  waiting for transfers between devices  330 us (88%)
  matrix products  30.8 us (8%)
  between operations  13.8 us (4%)
    all_gather x1, waiting for transfers between devices, body(): lax.all_gather(qkv_weight, 'gy', axis=0, tiled=True)  90.1 us
    reduce_scatter x1, waiting for transfers between devices, body(): lax.psum_scatter(lax.dot_general(input_rows, grad_rows, (((0,), (0,)), ((...  89.3 us
    all_gather x1, waiting for transfers between devices, body(): grads_all = lax.all_gather(qkv_grad, 'gx', axis=1, tiled=True)  77.9 us
    all_gather x1, waiting for transfers between devices, body(): inputs_all = lax.all_gather(layer_input, 'gz', axis=1, tiled=True)  36.2 us
    reduce_scatter x1, waiting for transfers between devices, body(): lax.psum_scatter(partial_value.astype(jnp.bfloat16), 'gz', scatter_dimens...  34.6 us
    dot_general x1, matrix products, body(): lax.dot_general(input_rows, grad_rows, (((0,), (0,)), ((), ())), preferre...  15.4 us
    dot_general x1, matrix products, body(): lax.dot_general(grad_rows, lax.all_gather(qkv_weight, 'gy', axis=0, tiled...  15.3 us
  transfers between devices with their start and end apart: 5, of which 5 were waited for; matrix products, arithmetic and copies ran while one was open for 8% of the time, Pallas kernels for 0%

commit v1 on v0

v1 whole, which is shorter than its diff:
```python
import jax
import jax.numpy as jnp
from jax import lax
from jax.experimental import pallas as pl
from jax.experimental.pallas import tpu as pltpu
from jax.sharding import PartitionSpec as P

MESH = pl.DeviceIdType.MESH
BF = jnp.bfloat16
F32 = jnp.float32
N = 2304
NMSG = 96


def m4(v):
    return lax.rem(v + 8, 4)


def swap12(v):
    return lax.div(v, 2) + 2 * lax.rem(v, 2)


def kernel(x_in, g_in, w_in, dx_out, dw_out, G, X, W, PB, RS, ACC, DWB, ssem, rsem, lsem, dsem):
    gx, gy, gz = lax.axis_index("gx"), lax.axis_index("gy"), lax.axis_index("gz")
    x_hi, z = lax.rem(gx, 2), lax.div(gx, 2)
    x_lo, c = lax.div(gy, 2), lax.rem(gy, 2)
    x, y, k = x_hi * 2 + x_lo, gz, gy
    oc = 1 - c
    xpair = x + 1 - 2 * x_lo

    def dev(dx=0, dy=0, dz=0):
        xx = m4(x + dx)
        return (m4(z + dz) * 2 + lax.div(xx, 2), lax.rem(xx, 2) * 2 + c, m4(y + dy))

    XP, XM, YP, YM, ZP, ZM = dev(dx=1), dev(dx=-1), dev(dy=1), dev(dy=-1), dev(dz=1), dev(dz=-1)
    SIB = (gx, x_lo * 2 + oc, y)
    PAIR = (gx, (1 - x_lo) * 2 + c, y)
    PAIRO = (gx, (1 - x_lo) * 2 + oc, y)
    is_self = jnp.logical_and(k == 0, y == 0)
    not_self = jnp.logical_not(is_self)
    TDST = (gx, swap12(m4(y - k)), k)
    TSRC = (gx, y, m4(y + swap12(k)))

    sends = []

    def send(src, dst, device):
        i = len(sends)
        copy = pltpu.make_async_remote_copy(
            src_ref=src,
            dst_ref=dst,
            send_sem=ssem.at[i],
            recv_sem=rsem.at[i],
            device_id=device,
            device_id_type=MESH,
        )
        sends.append(copy)
        copy.start()
        return copy

    def got(*copies):
        for copy in copies:
            copy.wait_recv()

    def shard(dz, dx, lo=0, rows=128, core=None):
        xx = m4(x + dx)
        slot = lax.rem(xx, 2) * 2 + lax.div(xx, 2)
        return G.at[m4(z + dz), c if core is None else core, slot, pl.ds(lo, rows)]

    def xcols(kk):
        return x_in.at[0, :, pl.ds(pl.multiple_of(kk * 512, 512), 512)]

    gs, gs_sib, gs_pair, gs_pairo = c * 2 + x_lo, oc * 2 + x_lo, c * 2 + 1 - x_lo, oc * 2 + 1 - x_lo

    def xslot(dy, g):
        return X.at[m4(y + dy), g]

    own_g = pltpu.make_async_copy(g_in.at[0], shard(0, 0), lsem.at[0])
    own_g.start()
    own_x = pltpu.make_async_copy(xcols(k), xslot(0, gs), lsem.at[1])
    own_x.start()
    own_w = pltpu.make_async_copy(w_in, W, lsem.at[2])
    own_w.start()

    barrier = pltpu.get_barrier_semaphore()
    for device in (XP, XM, YP, YM, ZP, ZM, SIB, PAIRO):
        pl.semaphore_signal(barrier, inc=1, device_id=device, device_id_type=MESH)

    @pl.when(not_self)
    def _():
        pl.semaphore_signal(barrier, inc=1, device_id=TDST, device_id_type=MESH)
        pl.semaphore_signal(barrier, inc=1, device_id=TSRC, device_id_type=MESH)

    pl.semaphore_wait(barrier, jnp.where(is_self, 8, 10))

    xa_pair = send(xcols(lax.rem(k + 2, 4)), xslot(0, gs), PAIR)
    xa_pairo = send(xcols(PAIRO[1]), xslot(0, gs), PAIRO)
    xa_sib = send(xcols(SIB[1]), xslot(0, gs), SIB)

    def own(lo, device):
        return send(g_in.at[0, pl.ds(lo, 64)], shard(0, 0, lo, 64), device)

    gxp0, gxm0, gzp0, gzm0 = own(0, XP), own(0, XM), own(0, ZP), own(0, ZM)
    xyp_own, xym_own = send(xcols(k), xslot(0, gs), YP), send(xcols(k), xslot(0, gs), YM)
    gxp1, gxm1, gzp1, gzm1 = own(64, XP), own(64, XM), own(64, ZP), own(64, ZM)

    def both(ref, plus, minus):
        return send(ref, ref, plus), send(ref, ref, minus)

    got(xa_sib)
    xyp_sib, xym_sib = both(xslot(0, gs_sib), YP, YM)

    got(gxp0)
    gxp2 = send(shard(0, -1, 0, 64), shard(0, -1, 0, 64), XP)
    zsp0, zsm0 = both(shard(0, -1, 0, 64), ZP, ZM)
    got(gzp0)
    gzp2 = send(shard(-1, 0, 0, 64), shard(-1, 0, 0, 64), ZP)
    got(gxm0)
    zsp1, zsm1 = both(shard(0, 1, 0, 64), ZP, ZM)
    got(gzm0)
    got(gzm1)
    gzm2 = send(shard(1, 0, 64, 64), shard(1, 0, 64, 64), ZM)
    xsp1, xsm1 = both(shard(1, 0, 64, 64), XP, XM)
    got(gxm1)
    gxm2 = send(shard(0, 1, 64, 64), shard(0, 1, 64, 64), XM)
    got(gzp1)
    xsp0, xsm0 = both(shard(-1, 0, 64, 64), XP, XM)
    got(gxp1)

    got(xa_pair)
    xyp_pair, xym_pair = both(xslot(0, gs_pair), YP, YM)
    got(xyp_own)
    xfp_own = send(xslot(-1, gs), xslot(-1, gs), YP)
    got(xa_pairo)
    xyp_pairo, xym_pairo = both(xslot(0, gs_pairo), YP, YM)
    got(xym_own)

    got(gxp2)
    zsp2, zsm2 = both(shard(0, 2, 0, 64), ZP, ZM)
    got(gzm2)
    xsp2, xsm2 = both(shard(2, 0, 64, 64), XP, XM)
    got(gxm2)
    own_g.wait()

    def to_sibling(dz):
        ref = G.at[m4(z + dz), c]
        return send(ref, ref, SIB)

    sib0 = to_sibling(0)
    own_w.wait()
    own_x.wait()

    def dx_half(r, dz, core):
        rows = G[m4(z + dz), core].reshape(512, N)
        part = lax.dot_general(rows, W[...], (((1,), (1,)), ((), ())), preferred_element_type=F32)
        PB[r, pl.ds(core * 2, 2)] = part.astype(BF).reshape(2, 2, 128, 512)

    def rs_first(r):
        return (
            send(PB.at[r, m4(y - 1 - k), 0], RS.at[r, 0, 0], YP),
            send(PB.at[r, m4(y + 1 - k), 1], RS.at[r, 1, 0], YM),
        )

    def rs_add(r, step):
        for way, land in ((0, m4(y - 2 - step - k)), (1, m4(y + 2 + step - k))):
            total = RS[r, way, step].astype(F32) + PB[r, land, way].astype(F32)
            RS[r, way, step] = total.astype(BF)

    def rs_next(r, step, copies):
        got(*copies)
        rs_add(r, step)
        return (
            send(RS.at[r, 0, step], RS.at[r, 0, step + 1], YP),
            send(RS.at[r, 1, step], RS.at[r, 1, step + 1], YM),
        )

    last = []

    def rs_last(r, dz, copies):
        got(*copies)
        rs_add(r, 2)
        zi = m4(z + dz)
        for way in range(2):
            row = pl.multiple_of(zi * 256 + way * 128, 128)
            dst = dx_out.at[0, pl.ds(row, 128)]
            i = len(sends) + len(last)
            remote = pltpu.make_async_remote_copy(
                src_ref=RS.at[r, way, 2],
                dst_ref=dst,
                send_sem=ssem.at[NMSG - 1 - len(last)],
                recv_sem=rsem.at[NMSG - 1 - len(last)],
                device_id=TDST,
                device_id_type=MESH,
            )
            local = pltpu.make_async_copy(RS.at[r, way, 2], dst, lsem.at[4 + len(last)])
            last.append((remote, local))
            pl.when(not_self)(remote.start)
            pl.when(is_self)(local.start)

    def dw_block(dz, mode, first=0, last_=3):
        zi = m4(z + dz)

        def tile(i, carry):
            cols = pl.ds(pl.multiple_of(i * 768, 768), 768)
            prod = lax.dot_general(
                X[zi].reshape(1024, 512),
                G[zi, :, :, :, cols].reshape(1024, 768),
                (((0,), (0,)), ((), ())),
                preferred_element_type=F32,
            )
            if mode == 0:
                ACC[:, cols] = prod
            elif mode == 1:
                ACC[:, cols] += prod
            else:
                DWB[:, cols] = (ACC[:, cols] + prod).astype(BF)
            return carry

        lax.fori_loop(first, last_, tile, 0)

    got(zsp0)
    ztp0 = send(shard(-1, -1, 0, 64), shard(-1, -1, 0, 64), ZP)
    got(zsm1)
    ztm1 = send(shard(1, 1, 0, 64), shard(1, 1, 0, 64), ZM)
    got(xsp0)
    xtp0 = send(shard(-1, -1, 64, 64), shard(-1, -1, 64, 64), XP)
    got(xsm1)
    xtm1 = send(shard(1, 1, 64, 64), shard(1, 1, 64, 64), XM)
    got(xym_sib)
    xfm_sib = send(xslot(1, gs_sib), xslot(1, gs_sib), YM)
    got(xyp_sib)

    dx_half(0, 0, c)
    got(sib0)
    dx_half(0, 0, oc)
    rs0 = rs_first(0)

    got(xyp_pair)
    xfp_pair = send(xslot(-1, gs_pair), xslot(-1, gs_pair), YP)
    got(xym_pairo)
    xfm_pairo = send(xslot(1, gs_pairo), xslot(1, gs_pairo), YM)

    got(zsp2)
    ztp2 = send(shard(-1, 2, 0, 32), shard(-1, 2, 0, 32), ZP)
    got(zsm2)
    ztm2 = send(shard(1, 2, 32, 32), shard(1, 2, 32, 32), ZM)
    got(xsp2)
    xtp2 = send(shard(2, -1, 64, 32), shard(2, -1, 64, 32), XP)
    got(xsm2)
    xtm2 = send(shard(2, 1, 96, 32), shard(2, 1, 96, 32), XM)

    rs0 = rs_next(0, 0, rs0)

    got(zsp1, xsm0, xtp0)
    sib1 = to_sibling(-1)
    got(zsm0, xsp1, xtm1)
    sib2 = to_sibling(1)
    rs0 = rs_next(0, 1, rs0)

    dx_half(1, -1, c)
    got(sib1)
    dx_half(1, -1, oc)
    rs1 = rs_first(1)
    dx_half(2, 1, c)
    got(sib2)
    dx_half(2, 1, oc)
    rs2 = rs_first(2)
    rs_last(0, 0, rs0)

    got(gzp2, ztp0, ztm1, ztp2, ztm2, xtp2, xtm2)
    sib3 = to_sibling(2)
    rs1 = rs_next(1, 0, rs1)
    dx_half(3, 2, c)
    rs2 = rs_next(2, 0, rs2)
    got(sib3)
    dx_half(3, 2, oc)
    rs3 = rs_first(3)
    rs1 = rs_next(1, 1, rs1)
    got(xym_pair, xyp_pairo, xfp_own, xfm_sib, xfp_pair, xfm_pairo)
    rs2 = rs_next(2, 1, rs2)
    dw_block(0, 0)
    rs3 = rs_next(3, 0, rs3)
    rs_last(1, -1, rs1)
    rs_last(2, 1, rs2)
    dw_block(-1, 1)
    rs3 = rs_next(3, 1, rs3)
    dw_block(1, 1)
    rs_last(3, 2, rs3)
    dw_block(2, 2)

    out = pltpu.make_async_copy(DWB, dw_out, dsem)
    out.start()
    for copy in sends:
        copy.wait_send()
    for remote, local in last:

        @pl.when(not_self)
        def _(remote=remote):
            remote.wait_send()
            remote.wait_recv()

        pl.when(is_self)(local.wait)
    out.wait()


def body(layer_input, qkv_grad, qkv_weight):
    anyspec = pl.BlockSpec(memory_space=pl.ANY)
    return pl.pallas_call(
        kernel,
        out_shape=(
            jax.ShapeDtypeStruct((1, 1024, 512), BF),
            jax.ShapeDtypeStruct((512, N), BF),
        ),
        in_specs=[anyspec] * 3,
        out_specs=(anyspec, anyspec),
        scratch_shapes=[
            pltpu.VMEM((4, 2, 4, 128, N), BF),
            pltpu.VMEM((4, 4, 256, 512), BF),
            pltpu.VMEM((512, N), BF),
            pltpu.VMEM((4, 4, 2, 128, 512), BF),
            pltpu.VMEM((4, 2, 3, 128, 512), BF),
            pltpu.VMEM((512, N), F32),
            pltpu.VMEM((512, N), BF),
            pltpu.SemaphoreType.DMA((NMSG,)),
            pltpu.SemaphoreType.DMA((NMSG,)),
            pltpu.SemaphoreType.DMA((16,)),
            pltpu.SemaphoreType.DMA,
        ],
        compiler_params=pltpu.CompilerParams(
            collective_id=1, has_side_effects=True, vmem_limit_bytes=60 * 2**20
        ),
        cost_estimate=pl.CostEstimate(
            flops=4 * 4096 * 512 * N, bytes_accessed=8 * 2**20, transcendentals=0
        ),
    )(layer_input, qkv_grad, qkv_weight)


def solution(mesh):
    return jax.shard_map(
        body,
        mesh=mesh,
        in_specs=(P("gy", "gz", "gx"), P("gy", "gx", "gz"), P(("gx", "gy"), "gz")),
        out_specs=(P("gy", None, ("gx", "gz")), P(("gx", "gy"), "gz")),
        check_vma=False,
    )
```

time: 377 us -> 124 us (0.33)
  the two profiles are of different devices: /device:TPU:3 before, /device:TPU:98 now
where the time goes in v1:
time: 124 us
  Pallas kernels  118 us (95%)
  local copies, waits for them, and re-layouts  5.48 us (4%)
    pallas_call x1, Pallas kernels, body(): pl.pallas_call(kernel, out_shape=(jax.ShapeDtypeStruct((1, 1024, 512), BF...  118 us
    unnamed x2, local copies, waits for them, and re-layouts  5.48 us

profile of v1, /device:TPU:98, one launch (start us, length us, event | category | flops | bytes accessed | tf_op | source)
XLA Modules:
  0.0 124.3 jit_solution(15179503729755978986)
XLA Ops:
  0.6 118.1 %shard_map.50 = (bf16[1,1024,512]{2,1,0:T(8,128)(2,1)}, bf16[512,2304]{1,0:T(8,128)(2,1)}) custom-call(bf16[1,256,2048]{2,1,0:T(8,128)(2,1)} %x_in.1, bf16[1,128,2304]{2,1,0:T(8,128)(2,1)} %g_in.1, bf16[512,2304]{1,0:T(8,128)(2,1)} %w_in.1), custom_call_target="tpu_custom_call" | custom-call | flops 19327352832 | bytes 8388608 | tf_op jit(solution)/shard_map/pallas_call | solution.py:307
  118.8 2.3 %copy.7 = bf16[1,1024,512]{2,1,0:T(8,128)(2,1)} copy(bf16[1,1024,512]{2,1,0:T(8,128)(2,1)} %get-tuple-element.4) | data formatting | bytes 2097152
  121.0 3.2 %copy.8 = bf16[512,2304]{1,0:T(8,128)(2,1)} copy(bf16[512,2304]{1,0:T(8,128)(2,1)} %get-tuple-element.5) | data formatting | bytes 4718592

commit v2 on v1

v2 whole, which is shorter than its diff:
```python
import jax
import jax.numpy as jnp
from jax import lax
from jax.experimental import pallas as pl
from jax.experimental.pallas import tpu as pltpu
from jax.sharding import PartitionSpec as P

MESH = pl.DeviceIdType.MESH
BF = jnp.bfloat16
F32 = jnp.float32
N = 2304
NMSG = 96
H0, H1 = 80, 48
H0A, H1A = 32, 32


def m4(v):
    return lax.rem(v + 8, 4)


def swap12(v):
    return lax.div(v, 2) + 2 * lax.rem(v, 2)


def kernel(x_in, g_in, w_in, dx_out, dw_out, G, X, W, PB, RS, ACC, DWB, ssem, rsem, lsem, dsem):
    gx, gy, gz = lax.axis_index("gx"), lax.axis_index("gy"), lax.axis_index("gz")
    x_hi, z = lax.rem(gx, 2), lax.div(gx, 2)
    x_lo, c = lax.div(gy, 2), lax.rem(gy, 2)
    x, y, k = x_hi * 2 + x_lo, gz, gy
    oc = 1 - c

    def dev(dx=0, dy=0, dz=0):
        xx = m4(x + dx)
        return (m4(z + dz) * 2 + lax.div(xx, 2), lax.rem(xx, 2) * 2 + c, m4(y + dy))

    to_p = 1 - 2 * x_lo
    XP, XQ = dev(dx=to_p), dev(dx=-to_p)
    YP, YM, ZP, ZM = dev(dy=1), dev(dy=-1), dev(dz=1), dev(dz=-1)
    SIB = (gx, x_lo * 2 + oc, y)
    PAIRO = (gx, (1 - x_lo) * 2 + oc, y)
    is_self = jnp.logical_and(k == 0, y == 0)
    not_self = jnp.logical_not(is_self)
    TDST = (gx, swap12(m4(y - k)), k)
    TSRC = (gx, y, m4(y + swap12(k)))

    sends = []

    def send(src, dst, device):
        i = len(sends)
        copy = pltpu.make_async_remote_copy(
            src_ref=src,
            dst_ref=dst,
            send_sem=ssem.at[i],
            recv_sem=rsem.at[i],
            device_id=device,
            device_id_type=MESH,
        )
        sends.append(copy)
        copy.start()
        return copy

    def got(*copies):
        for copy in copies:
            copy.wait_recv()

    def shard(dz, dx, lo=0, rows=128, core=None):
        xx = m4(x + dx)
        slot = lax.rem(xx, 2) * 2 + lax.div(xx, 2)
        return G.at[m4(z + dz), c if core is None else core, slot, pl.ds(lo, rows)]

    def xcols(kk):
        return x_in.at[0, :, pl.ds(pl.multiple_of(kk * 512, 512), 512)]

    gs, gs_sib, gs_pair, gs_pairo = c * 2 + x_lo, oc * 2 + x_lo, c * 2 + 1 - x_lo, oc * 2 + 1 - x_lo

    def xslot(dy, g):
        return X.at[m4(y + dy), g]

    own_g = pltpu.make_async_copy(g_in.at[0], shard(0, 0), lsem.at[0])
    own_g.start()
    own_x = pltpu.make_async_copy(xcols(k), xslot(0, gs), lsem.at[1])
    own_x.start()
    own_w = pltpu.make_async_copy(w_in, W, lsem.at[2])
    own_w.start()

    barrier = pltpu.get_barrier_semaphore()
    for device in (XP, XQ, YP, YM, ZP, ZM, SIB, PAIRO):
        pl.semaphore_signal(barrier, inc=1, device_id=device, device_id_type=MESH)

    @pl.when(not_self)
    def _():
        pl.semaphore_signal(barrier, inc=1, device_id=TDST, device_id_type=MESH)
        pl.semaphore_signal(barrier, inc=1, device_id=TSRC, device_id_type=MESH)

    pl.semaphore_wait(barrier, jnp.where(is_self, 8, 10))

    def own(lo, rows, device):
        return send(g_in.at[0, pl.ds(lo, rows)], shard(0, 0, lo, rows), device)

    gp0, gq0, gzp0, gzm0 = own(0, H0, XP), own(0, H0, XQ), own(0, H0, ZP), own(0, H0, ZM)
    xyp_own, xym_own = send(xcols(k), xslot(0, gs), YP), send(xcols(k), xslot(0, gs), YM)
    xa_sib = send(xcols(SIB[1]), xslot(0, gs), SIB)
    xa_pair = send(xcols(XP[1]), xslot(0, gs), XP)
    gq1, gzp1, gzm1 = own(H0, H1, XQ), own(H0, H1, ZP), own(H0, H1, ZM)

    def both(ref, plus, minus):
        return send(ref, ref, plus), send(ref, ref, minus)

    def to_sibling(dz, lo, rows):
        ref = G.at[m4(z + dz), c, :, pl.ds(lo, rows)]
        return send(ref, ref, SIB)

    def on(ref, device):
        return send(ref, ref, device)

    def dx_half(r, dz, core):
        rows = G[m4(z + dz), core].reshape(512, N)
        part = lax.dot_general(rows, W[...], (((1,), (1,)), ((), ())), preferred_element_type=F32)
        PB[r, pl.ds(core * 2, 2)] = part.astype(BF).reshape(2, 2, 128, 512)

    def land(dy):
        return m4(y + dy - k)

    def rs_start(r):
        return (
            send(PB.at[r, land(2), 0], RS.at[r, 0, 0], YP),
            send(PB.at[r, land(2), 1], RS.at[r, 1, 0], YM),
            send(PB.at[r, land(1), 1], RS.at[r, 0, 1], YP),
            send(PB.at[r, land(-1), 0], RS.at[r, 1, 1], YM),
        )

    def rs_mid(r, copies):
        done = []
        for way, dy, device in ((0, 1, YP), (1, -1, YM)):
            got(copies[way])
            total = RS[r, way, 0].astype(F32) + PB[r, land(dy), way].astype(F32)
            RS[r, way, 0] = total.astype(BF)
            done.append(send(RS.at[r, way, 0], RS.at[r, way, 2], device))
        return (copies[2], copies[3], *done)

    last = []

    def rs_end(r, dz, copies):
        got(*copies)
        zi = m4(z + dz)
        for way in range(2):
            total = PB[r, land(0), way].astype(F32) + RS[r, 1 - way, 1].astype(F32)
            RS[r, way, 2] = (total + RS[r, way, 2].astype(F32)).astype(BF)
            row = pl.multiple_of(zi * 256 + way * 128, 128)
            dst = dx_out.at[0, pl.ds(row, 128)]
            remote = pltpu.make_async_remote_copy(
                src_ref=RS.at[r, way, 2],
                dst_ref=dst,
                send_sem=ssem.at[NMSG - 1 - len(last)],
                recv_sem=rsem.at[NMSG - 1 - len(last)],
                device_id=TDST,
                device_id_type=MESH,
            )
            local = pltpu.make_async_copy(RS.at[r, way, 2], dst, lsem.at[4 + len(last)])
            last.append((remote, local))
            pl.when(not_self)(remote.start)
            pl.when(is_self)(local.start)

    def dw_block(dz, mode, first=0, stop=3):
        zi = m4(z + dz)

        def tile(i, carry):
            cols = pl.ds(pl.multiple_of(i * 768, 768), 768)
            prod = lax.dot_general(
                X[zi].reshape(1024, 512),
                G[zi, :, :, :, cols].reshape(1024, 768),
                (((0,), (0,)), ((), ())),
                preferred_element_type=F32,
            )
            if mode == 0:
                ACC[:, cols] = prod
            elif mode == 1:
                ACC[:, cols] += prod
            else:
                DWB[:, cols] = (ACC[:, cols] + prod).astype(BF)
            return carry

        lax.fori_loop(first, stop, tile, 0)

    P_, Q_ = to_p, -to_p
    got(xa_sib)
    xyp_sib, xym_sib = both(xslot(0, gs_sib), YP, YM)
    got(gq0)
    gp1 = own(H0, H1, XP)
    zsp1, zsm1 = both(shard(0, Q_, 0, H0), ZP, ZM)
    got(xyp_own, xym_own)
    xfp_own = on(xslot(-1, gs), YP)
    got(xyp_sib, xym_sib)
    xfm_sib = on(xslot(1, gs_sib), YM)

    got(gp0)
    gf0 = on(shard(0, P_, 0, H0), XQ)
    zsp0, zsm0 = both(shard(0, P_, 0, H0), ZP, ZM)
    xa_pairo = send(xcols(PAIRO[1]), xslot(0, gs), PAIRO)
    got(xa_pair)
    xyp_pair, xym_pair = both(xslot(0, gs_pair), YP, YM)
    got(gp1)
    gf1 = on(shard(0, P_, H0, H1), XQ)
    got(gq1, gzp0, gzm0)

    got(gf0)
    own_g.wait()
    sib0a = to_sibling(0, 0, H0)
    zsp2, zsm2 = both(shard(0, 2, 0, H0), ZP, ZM)
    got(gzp1)
    xsp0, xsq0 = both(shard(-1, 0, H0, H1), XP, XQ)
    got(gzm1)
    xsp1, xsq1 = both(shard(1, 0, H0, H1), XP, XQ)
    got(xa_pairo)
    xyp_pairo, xym_pairo = both(xslot(0, gs_pairo), YP, YM)
    got(xyp_pair, xym_pair)
    xfp_pair = on(xslot(-1, gs_pair), YP)
    got(gf1)
    sib0b = to_sibling(0, H0, H1)

    own_w.wait()
    own_x.wait()
    dx_half(0, 0, c)
    got(zsp0, zsm0, zsp1, zsm1)
    gzp2 = on(shard(-1, 0, 0, H0), ZP)
    gzm2 = on(shard(1, 0, H0, H1), ZM)
    got(sib0a, sib0b)
    dx_half(0, 0, oc)
    rs0 = rs_start(0)

    got(xsp0)
    xt0 = on(shard(-1, P_, H0, H1), XQ)
    got(xsq1)
    xt1 = on(shard(1, Q_, H0, H1), XP)
    got(zsp2, zsm2)
    sib1a, sib2a = to_sibling(-1, 0, H0), to_sibling(1, 0, H0)
    ztp0, ztm1 = on(shard(-1, P_, 0, H0), ZP), on(shard(1, Q_, 0, H0), ZM)
    got(xym_pairo, xyp_pairo)
    xfm_pairo = on(xslot(1, gs_pairo), YM)
    rs0 = rs_mid(0, rs0)
    got(xsq0, xt0)
    sib1b = to_sibling(-1, H0, H1)
    got(xsp1, xt1)
    sib2b = to_sibling(1, H0, H1)
    got(gzm2)
    xsp2, xsq2 = both(shard(2, 0, H0, H1), XP, XQ)
    ztp2, ztm2 = on(shard(-1, 2, 0, H0A), ZP), on(shard(1, 2, H0A, H0 - H0A), ZM)
    dx_half(1, -1, c)
    got(sib1a, sib1b)
    dx_half(1, -1, oc)
    rs1 = rs_start(1)
    dx_half(2, 1, c)
    got(sib2a, sib2b)
    dx_half(2, 1, oc)
    rs2 = rs_start(2)

    got(xsp2)
    xt2a = on(shard(2, P_, H0, H1A), XQ)
    got(xsq2)
    xt2b = on(shard(2, Q_, H0 + H1A, H1 - H1A), XP)
    rs_end(0, 0, rs0)
    rs1 = rs_mid(1, rs1)
    got(gzp2, ztp0, ztm1, ztp2, ztm2)
    sib3a = to_sibling(2, 0, H0)
    got(xfp_own, xfm_sib, xfp_pair, xfm_pairo)
    dw_block(0, 0, 0, 2)
    got(xt2a, xt2b)
    sib3b = to_sibling(2, H0, H1)
    rs2 = rs_mid(2, rs2)
    dx_half(3, 2, c)
    got(sib3a, sib3b)
    dx_half(3, 2, oc)
    rs3 = rs_start(3)
    dw_block(0, 0, 2)
    dw_block(-1, 1, 0, 2)
    rs3 = rs_mid(3, rs3)
    rs_end(1, -1, rs1)
    rs_end(2, 1, rs2)
    dw_block(-1, 1, 2)
    dw_block(1, 1)
    rs_end(3, 2, rs3)
    dw_block(2, 2)

    out = pltpu.make_async_copy(DWB, dw_out, dsem)
    out.start()
    for copy in sends:
        copy.wait_send()
    for remote, local in last:

        @pl.when(not_self)
        def _(remote=remote):
            remote.wait_send()
            remote.wait_recv()

        pl.when(is_self)(local.wait)
    out.wait()


def copy_kernel(a_in, b_in, a_out, b_out, a_buf, b_buf, in_sem, out_sem):
    parts = []
    for i in range(4):
        rows = pl.ds(i * 128, 128)
        parts.append((b_in.at[rows], b_buf.at[rows], b_out.at[rows]))
    for i in range(4):
        rows = pl.ds(i * 256, 256)
        parts.append((a_in.at[0, rows], a_buf.at[rows], a_out.at[0, rows]))
    reads = [pltpu.make_async_copy(p[0], p[1], in_sem.at[i]) for i, p in enumerate(parts)]
    writes = [pltpu.make_async_copy(p[1], p[2], out_sem.at[i]) for i, p in enumerate(parts)]
    for read in reads:
        read.start()
    for read, write in zip(reads, writes):
        read.wait()
        write.start()
    for write in writes:
        write.wait()


def body(layer_input, qkv_grad, qkv_weight):
    anyspec = pl.BlockSpec(memory_space=pl.ANY)
    results = pl.pallas_call(
        kernel,
        out_shape=(
            jax.ShapeDtypeStruct((1, 1024, 512), BF),
            jax.ShapeDtypeStruct((512, N), BF),
        ),
        in_specs=[anyspec] * 3,
        out_specs=(anyspec, anyspec),
        scratch_shapes=[
            pltpu.VMEM((4, 2, 4, 128, N), BF),
            pltpu.VMEM((4, 4, 256, 512), BF),
            pltpu.VMEM((512, N), BF),
            pltpu.VMEM((4, 4, 2, 128, 512), BF),
            pltpu.VMEM((4, 2, 3, 128, 512), BF),
            pltpu.VMEM((512, N), F32),
            pltpu.VMEM((512, N), BF),
            pltpu.SemaphoreType.DMA((NMSG,)),
            pltpu.SemaphoreType.DMA((NMSG,)),
            pltpu.SemaphoreType.DMA((16,)),
            pltpu.SemaphoreType.DMA,
        ],
        compiler_params=pltpu.CompilerParams(
            collective_id=1, has_side_effects=True, vmem_limit_bytes=60 * 2**20
        ),
        cost_estimate=pl.CostEstimate(
            flops=4 * 4096 * 512 * N, bytes_accessed=8 * 2**20, transcendentals=0
        ),
    )(layer_input, qkv_grad, qkv_weight)
    return pl.pallas_call(
        copy_kernel,
        out_shape=tuple(jax.ShapeDtypeStruct(r.shape, BF) for r in results),
        in_specs=[anyspec] * 2,
        out_specs=(anyspec, anyspec),
        scratch_shapes=[
            pltpu.VMEM((1024, 512), BF),
            pltpu.VMEM((512, N), BF),
            pltpu.SemaphoreType.DMA((8,)),
            pltpu.SemaphoreType.DMA((8,)),
        ],
        compiler_params=pltpu.CompilerParams(vmem_limit_bytes=60 * 2**20),
        cost_estimate=pl.CostEstimate(flops=0, bytes_accessed=7 * 2**20, transcendentals=0),
    )(*results)


def solution(mesh):
    return jax.shard_map(
        body,
        mesh=mesh,
        in_specs=(P("gy", "gz", "gx"), P("gy", "gx", "gz"), P(("gx", "gy"), "gz")),
        out_specs=(P("gy", None, ("gx", "gz")), P(("gx", "gy"), "gz")),
        check_vma=False,
    )
```

time: 124 us -> 103 us (0.83)
  the two profiles are of different devices: /device:TPU:98 before, /device:TPU:3 now
where the time goes in v2:
time: 103 us; the launch traced here: 102 us
  Pallas kernels  102 us (99%)
    pallas_call x1, Pallas kernels, body(): pl.pallas_call(kernel, out_shape=(jax.ShapeDtypeStruct((1, 1024, 512), BF...  98.6 us
    pallas_call x1, Pallas kernels, body(): pl.pallas_call(copy_kernel, out_shape=tuple((jax.ShapeDtypeStruct(r.shape...  2.94 us

profile of v2, /device:TPU:3, one launch (start us, length us, event | category | flops | bytes accessed | tf_op | source)
XLA Modules:
  0.0 102.4 jit_solution(1214514908166701442)
XLA Ops:
  0.6 98.6 %shard_map.50 = (bf16[1,1024,512]{2,1,0:T(8,128)(2,1)}, bf16[512,2304]{1,0:T(8,128)(2,1)}) custom-call(bf16[1,256,2048]{2,1,0:T(8,128)(2,1)} %x_in.1, bf16[1,128,2304]{2,1,0:T(8,128)(2,1)} %g_in.1, bf16[512,2304]{1,0:T(8,128)(2,1)} %w_in.1), custom_call_target="tpu_custom_call" | custom-call | flops 19327352832 | bytes 8388608 | tf_op jit(solution)/shard_map/pallas_call | solution.py:320
  99.3 2.9 %shard_map.51 = (bf16[1,1024,512]{2,1,0:T(8,128)(2,1)}, bf16[512,2304]{1,0:T(8,128)(2,1)}) custom-call(bf16[1,1024,512]{2,1,0:T(8,128)(2,1)} %get-tuple-element.4.a_in, bf16[512,2304]{1,0:T(8,128)(2,1)} %get-tuple-element.5.b_in), custom_call_target="tpu_custom_call" | custom-call | bytes 7340032 | tf_op jit(solution)/shard_map/pallas_call | solution.py:348

commit v3 on v2

--- a/solution.py
+++ b/solution.py
@@ -9,7 +9,8 @@
 BF = jnp.bfloat16
 F32 = jnp.float32
 N = 2304
-NMSG = 96
+NMSG = 128
+TILE = 2304
 H0, H1 = 80, 48
 H0A, H1A = 32, 32
 
@@ -22,7 +23,7 @@
     return lax.div(v, 2) + 2 * lax.rem(v, 2)
 
 
-def kernel(x_in, g_in, w_in, dx_out, dw_out, G, X, W, PB, RS, ACC, DWB, ssem, rsem, lsem, dsem):
+def kernel(x_in, g_in, w_in, dx_out, dw_out, G, X, W, PB0, PB1, RS0, RS1, ACC, DWB, ssem, rsem, lsem, dsem):
     gx, gy, gz = lax.axis_index("gx"), lax.axis_index("gy"), lax.axis_index("gz")
     x_hi, z = lax.rem(gx, 2), lax.div(gx, 2)
     x_lo, c = lax.div(gy, 2), lax.rem(gy, 2)
@@ -113,62 +114,69 @@
     def on(ref, device):
         return send(ref, ref, device)
 
-    def dx_half(r, dz, core):
-        rows = G[m4(z + dz), core].reshape(512, N)
+    DZ = (0, -1, 1, 2)
+    PB, RS, LO, ROWS = (PB0, PB1), (RS0, RS1), (0, H0), (H0, H1)
+
+    def dx_part(h, r, core, cores=1):
+        n = ROWS[h]
+        rows = G[m4(z + DZ[r]), pl.ds(core, cores), :, pl.ds(LO[h], n), :].reshape(cores * 4 * n, N)
         part = lax.dot_general(rows, W[...], (((1,), (1,)), ((), ())), preferred_element_type=F32)
-        PB[r, pl.ds(core * 2, 2)] = part.astype(BF).reshape(2, 2, 128, 512)
+        PB[h][r, pl.ds(core * 2, cores * 2)] = part.astype(BF).reshape(cores * 2, 2, n, 512)
 
     def land(dy):
         return m4(y + dy - k)
 
-    def rs_start(r):
+    def rs_start(h, r, nr):
+        rr, pb, rs = pl.ds(r, nr), PB[h], RS[h]
         return (
-            send(PB.at[r, land(2), 0], RS.at[r, 0, 0], YP),
-            send(PB.at[r, land(2), 1], RS.at[r, 1, 0], YM),
-            send(PB.at[r, land(1), 1], RS.at[r, 0, 1], YP),
-            send(PB.at[r, land(-1), 0], RS.at[r, 1, 1], YM),
+            send(pb.at[rr, land(2), 0], rs.at[rr, 0, 0], YP),
+            send(pb.at[rr, land(2), 1], rs.at[rr, 1, 0], YM),
+            send(pb.at[rr, land(1), 1], rs.at[rr, 0, 1], YP),
+            send(pb.at[rr, land(-1), 0], rs.at[rr, 1, 1], YM),
         )
 
-    def rs_mid(r, copies):
+    def rs_mid(h, r, nr, copies):
+        rr, pb, rs = pl.ds(r, nr), PB[h], RS[h]
         done = []
         for way, dy, device in ((0, 1, YP), (1, -1, YM)):
             got(copies[way])
-            total = RS[r, way, 0].astype(F32) + PB[r, land(dy), way].astype(F32)
-            RS[r, way, 0] = total.astype(BF)
-            done.append(send(RS.at[r, way, 0], RS.at[r, way, 2], device))
+            total = rs[rr, way, 0].astype(F32) + pb[rr, land(dy), way].astype(F32)
+            rs[rr, way, 0] = total.astype(BF)
+            done.append(send(rs.at[rr, way, 0], rs.at[rr, way, 2], device))
         return (copies[2], copies[3], *done)
 
     last = []
 
-    def rs_end(r, dz, copies):
+    def rs_end(h, r, nr, copies):
+        rr, pb, rs = pl.ds(r, nr), PB[h], RS[h]
         got(*copies)
+        for way in range(2):
+            total = pb[rr, land(0), way].astype(F32) + rs[rr, 1 - way, 1].astype(F32)
+            rs[rr, way, 2] = (total + rs[rr, way, 2].astype(F32)).astype(BF)
+            for q in range(r, r + nr):
+                row = pl.multiple_of(m4(z + DZ[q]) * 256 + way * 128 + LO[h], 16)
+                src, dst = rs.at[q, way, 2], dx_out.at[0, pl.ds(row, ROWS[h])]
+                remote = pltpu.make_async_remote_copy(
+                    src_ref=src,
+                    dst_ref=dst,
+                    send_sem=ssem.at[NMSG - 1 - len(last)],
+                    recv_sem=rsem.at[NMSG - 1 - len(last)],
+                    device_id=TDST,
+                    device_id_type=MESH,
+                )
+                local = pltpu.make_async_copy(src, dst, lsem.at[4 + len(last)])
+                last.append((remote, local))
+                pl.when(not_self)(remote.start)
+                pl.when(is_self)(local.start)
+
+    def dw_block(dz, mode):
         zi = m4(z + dz)
-        for way in range(2):
-            total = PB[r, land(0), way].astype(F32) + RS[r, 1 - way, 1].astype(F32)
-            RS[r, way, 2] = (total + RS[r, way, 2].astype(F32)).astype(BF)
-            row = pl.multiple_of(zi * 256 + way * 128, 128)
-            dst = dx_out.at[0, pl.ds(row, 128)]
-            remote = pltpu.make_async_remote_copy(
-                src_ref=RS.at[r, way, 2],
-                dst_ref=dst,
-                send_sem=ssem.at[NMSG - 1 - len(last)],
-                recv_sem=rsem.at[NMSG - 1 - len(last)],
-                device_id=TDST,
-                device_id_type=MESH,
-            )
-            local = pltpu.make_async_copy(RS.at[r, way, 2], dst, lsem.at[4 + len(last)])
-            last.append((remote, local))
-            pl.when(not_self)(remote.start)
-            pl.when(is_self)(local.start)
-
-    def dw_block(dz, mode, first=0, stop=3):
-        zi = m4(z + dz)
 
         def tile(i, carry):
-            cols = pl.ds(pl.multiple_of(i * 768, 768), 768)
+            cols = pl.ds(pl.multiple_of(i * TILE, 128), TILE)
             prod = lax.dot_general(
                 X[zi].reshape(1024, 512),
-                G[zi, :, :, :, cols].reshape(1024, 768),
+                G[zi, :, :, :, cols].reshape(1024, TILE),
                 (((0,), (0,)), ((), ())),
                 preferred_element_type=F32,
             )
@@ -180,7 +188,7 @@
                 DWB[:, cols] = (ACC[:, cols] + prod).astype(BF)
             return carry
 
-        lax.fori_loop(first, stop, tile, 0)
+        tile(0, 0)
 
     P_, Q_ = to_p, -to_p
     got(xa_sib)
@@ -211,33 +219,41 @@
     xsp0, xsq0 = both(shard(-1, 0, H0, H1), XP, XQ)
     got(gzm1)
     xsp1, xsq1 = both(shard(1, 0, H0, H1), XP, XQ)
+    own_w.wait()
+    own_x.wait()
+    dx_part(0, 0, c)
     got(xa_pairo)
     xyp_pairo, xym_pairo = both(xslot(0, gs_pairo), YP, YM)
+    got(sib0a)
+    dx_part(0, 0, oc)
+    s0a = rs_start(0, 0, 1)
+    got(gf1)
+    sib0b = to_sibling(0, H0, H1)
     got(xyp_pair, xym_pair)
     xfp_pair = on(xslot(-1, gs_pair), YP)
-    got(gf1)
-    sib0b = to_sibling(0, H0, H1)
-
-    own_w.wait()
-    own_x.wait()
-    dx_half(0, 0, c)
     got(zsp0, zsm0, zsp1, zsm1)
     gzp2 = on(shard(-1, 0, 0, H0), ZP)
     gzm2 = on(shard(1, 0, H0, H1), ZM)
-    got(sib0a, sib0b)
-    dx_half(0, 0, oc)
-    rs0 = rs_start(0)
-
+    got(sib0b)
+    dx_part(1, 0, 0, 2)
+    s0b = rs_start(1, 0, 1)
     got(xsp0)
     xt0 = on(shard(-1, P_, H0, H1), XQ)
-    got(xsq1)
-    xt1 = on(shard(1, Q_, H0, H1), XP)
+    got(xym_pairo, xyp_pairo)
+    xfm_pairo = on(xslot(1, gs_pairo), YM)
+    s0a = rs_mid(0, 0, 1, s0a)
     got(zsp2, zsm2)
     sib1a, sib2a = to_sibling(-1, 0, H0), to_sibling(1, 0, H0)
     ztp0, ztm1 = on(shard(-1, P_, 0, H0), ZP), on(shard(1, Q_, 0, H0), ZM)
-    got(xym_pairo, xyp_pairo)
-    xfm_pairo = on(xslot(1, gs_pairo), YM)
-    rs0 = rs_mid(0, rs0)
+    got(xsq1)
+    xt1 = on(shard(1, Q_, H0, H1), XP)
+    dx_part(0, 1, c)
+    dx_part(0, 2, c)
+    s0b = rs_mid(1, 0, 1, s0b)
+    got(sib1a, sib2a)
+    dx_part(0, 1, oc)
+    dx_part(0, 2, oc)
+    s1a = rs_start(0, 1, 2)
     got(xsq0, xt0)
     sib1b = to_sibling(-1, H0, H1)
     got(xsp1, xt1)
@@ -245,41 +261,41 @@
     got(gzm2)
     xsp2, xsq2 = both(shard(2, 0, H0, H1), XP, XQ)
     ztp2, ztm2 = on(shard(-1, 2, 0, H0A), ZP), on(shard(1, 2, H0A, H0 - H0A), ZM)
-    dx_half(1, -1, c)
-    got(sib1a, sib1b)
-    dx_half(1, -1, oc)
-    rs1 = rs_start(1)
-    dx_half(2, 1, c)
-    got(sib2a, sib2b)
-    dx_half(2, 1, oc)
-    rs2 = rs_start(2)
-
+    rs_end(0, 0, 1, s0a)
+    got(sib1b)
+    dx_part(1, 1, 0, 2)
+    got(sib2b)
+    dx_part(1, 2, 0, 2)
+    s1b = rs_start(1, 1, 2)
+    s1a = rs_mid(0, 1, 2, s1a)
     got(xsp2)
     xt2a = on(shard(2, P_, H0, H1A), XQ)
     got(xsq2)
     xt2b = on(shard(2, Q_, H0 + H1A, H1 - H1A), XP)
-    rs_end(0, 0, rs0)
-    rs1 = rs_mid(1, rs1)
+    got(xfp_own, xfm_sib, xfp_pair, xfm_pairo)
+    dw_block(0, 0)
+    got(xt2a, xt2b)
+    sib3b = to_sibling(2, H0, H1)
+    rs_end(1, 0, 1, s0b)
+    s1b = rs_mid(1, 1, 2, s1b)
     got(gzp2, ztp0, ztm1, ztp2, ztm2)
     sib3a = to_sibling(2, 0, H0)
-    got(xfp_own, xfm_sib, xfp_pair, xfm_pairo)
-    dw_block(0, 0, 0, 2)
-    got(xt2a, xt2b)
-    sib3b = to_sibling(2, H0, H1)
-    rs2 = rs_mid(2, rs2)
-    dx_half(3, 2, c)
-    got(sib3a, sib3b)
-    dx_half(3, 2, oc)
-    rs3 = rs_start(3)
-    dw_block(0, 0, 2)
-    dw_block(-1, 1, 0, 2)
-    rs3 = rs_mid(3, rs3)
-    rs_end(1, -1, rs1)
-    rs_end(2, 1, rs2)
-    dw_block(-1, 1, 2)
+    got(sib3b)
+    dx_part(1, 3, 0, 2)
+    s2b = rs_start(1, 3, 1)
+    dx_part(0, 3, c)
+    got(sib3a)
+    dx_part(0, 3, oc)
+    s2a = rs_start(0, 3, 1)
+    dw_block(-1, 1)
+    rs_end(0, 1, 2, s1a)
+    s2b = rs_mid(1, 3, 1, s2b)
+    s2a = rs_mid(0, 3, 1, s2a)
     dw_block(1, 1)
-    rs_end(3, 2, rs3)
+    rs_end(1, 1, 2, s1b)
+    rs_end(1, 3, 1, s2b)
     dw_block(2, 2)
+    rs_end(0, 3, 1, s2a)
 
     out = pltpu.make_async_copy(DWB, dw_out, dsem)
     out.start()
@@ -329,13 +345,15 @@
             pltpu.VMEM((4, 2, 4, 128, N), BF),
             pltpu.VMEM((4, 4, 256, 512), BF),
             pltpu.VMEM((512, N), BF),
-            pltpu.VMEM((4, 4, 2, 128, 512), BF),
-            pltpu.VMEM((4, 2, 3, 128, 512), BF),
+            pltpu.VMEM((4, 4, 2, H0, 512), BF),
+            pltpu.VMEM((4, 4, 2, H1, 512), BF),
+            pltpu.VMEM((4, 2, 3, H0, 512), BF),
+            pltpu.VMEM((4, 2, 3, H1, 512), BF),
             pltpu.VMEM((512, N), F32),
             pltpu.VMEM((512, N), BF),
             pltpu.SemaphoreType.DMA((NMSG,)),
             pltpu.SemaphoreType.DMA((NMSG,)),
-            pltpu.SemaphoreType.DMA((16,)),
+            pltpu.SemaphoreType.DMA((20,)),
             pltpu.SemaphoreType.DMA,
         ],
         compiler_params=pltpu.CompilerParams(

time: 103 us -> 100 us (0.971)
  Pallas kernels: 102 us -> 99.6 us
    pallas_call x1, Pallas kernels: 98.6 us -> 96.6 us  [body(): pl.pallas_call(kernel, out_shape=(jax.ShapeDtypeStruct((1, 1024, 512), BF...]
where the time goes in v3:
time: 100 us
  Pallas kernels  99.6 us (100%)
    pallas_call x1, Pallas kernels, body(): pl.pallas_call(kernel, out_shape=(jax.ShapeDtypeStruct((1, 1024, 512), BF...  96.6 us
    pallas_call x1, Pallas kernels, body(): pl.pallas_call(copy_kernel, out_shape=tuple((jax.ShapeDtypeStruct(r.shape...  2.94 us

profile of v3, /device:TPU:3, one launch (start us, length us, event | category | flops | bytes accessed | tf_op | source)
XLA Modules:
  0.0 100.4 jit_solution(7816347879743528948)
XLA Ops:
  0.6 96.6 %shard_map.50 = (bf16[1,1024,512]{2,1,0:T(8,128)(2,1)}, bf16[512,2304]{1,0:T(8,128)(2,1)}) custom-call(bf16[1,256,2048]{2,1,0:T(8,128)(2,1)} %x_in.1, bf16[1,128,2304]{2,1,0:T(8,128)(2,1)} %g_in.1, bf16[512,2304]{1,0:T(8,128)(2,1)} %w_in.1), custom_call_target="tpu_custom_call" | custom-call | flops 19327352832 | bytes 8388608 | tf_op jit(solution)/shard_map/pallas_call | solution.py:336
  97.3 2.9 %shard_map.51 = (bf16[1,1024,512]{2,1,0:T(8,128)(2,1)}, bf16[512,2304]{1,0:T(8,128)(2,1)}) custom-call(bf16[1,1024,512]{2,1,0:T(8,128)(2,1)} %get-tuple-element.4.a_in, bf16[512,2304]{1,0:T(8,128)(2,1)} %get-tuple-element.5.b_in), custom_call_target="tpu_custom_call" | custom-call | bytes 7340032 | tf_op jit(solution)/shard_map/pallas_call | solution.py:366

commit v4 on v3

--- a/solution.py
+++ b/solution.py
@@ -295,10 +295,10 @@
     rs_end(1, 1, 2, s1b)
     rs_end(1, 3, 1, s2b)
     dw_block(2, 2)
-    rs_end(0, 3, 1, s2a)
-
     out = pltpu.make_async_copy(DWB, dw_out, dsem)
     out.start()
+    rs_end(0, 3, 1, s2a)
+
     for copy in sends:
         copy.wait_send()
     for remote, local in last:
@@ -314,8 +314,8 @@
 
 def copy_kernel(a_in, b_in, a_out, b_out, a_buf, b_buf, in_sem, out_sem):
     parts = []
-    for i in range(4):
-        rows = pl.ds(i * 128, 128)
+    for i in range(8):
+        rows = pl.ds(i * 64, 64)
         parts.append((b_in.at[rows], b_buf.at[rows], b_out.at[rows]))
     for i in range(4):
         rows = pl.ds(i * 256, 256)
@@ -371,8 +371,8 @@
         scratch_shapes=[
             pltpu.VMEM((1024, 512), BF),
             pltpu.VMEM((512, N), BF),
-            pltpu.SemaphoreType.DMA((8,)),
-            pltpu.SemaphoreType.DMA((8,)),
+            pltpu.SemaphoreType.DMA((12,)),
+            pltpu.SemaphoreType.DMA((12,)),
         ],
         compiler_params=pltpu.CompilerParams(vmem_limit_bytes=60 * 2**20),
         cost_estimate=pl.CostEstimate(flops=0, bytes_accessed=7 * 2**20, transcendentals=0),

time: 100 us -> 100 us (level)
  no operation moved by 1% of the time
where the time goes in v4:
time: 100 us
  Pallas kernels  99.5 us (100%)
    pallas_call x1, Pallas kernels, body(): pl.pallas_call(kernel, out_shape=(jax.ShapeDtypeStruct((1, 1024, 512), BF...  96.6 us
    pallas_call x1, Pallas kernels, body(): pl.pallas_call(copy_kernel, out_shape=tuple((jax.ShapeDtypeStruct(r.shape...  2.93 us

profile of v4, /device:TPU:3, one launch (start us, length us, event | category | flops | bytes accessed | tf_op | source)
XLA Modules:
  0.0 100.3 jit_solution(5941228988895202014)
XLA Ops:
  0.6 96.6 %shard_map.50 = (bf16[1,1024,512]{2,1,0:T(8,128)(2,1)}, bf16[512,2304]{1,0:T(8,128)(2,1)}) custom-call(bf16[1,256,2048]{2,1,0:T(8,128)(2,1)} %x_in.1, bf16[1,128,2304]{2,1,0:T(8,128)(2,1)} %g_in.1, bf16[512,2304]{1,0:T(8,128)(2,1)} %w_in.1), custom_call_target="tpu_custom_call" | custom-call | flops 19327352832 | bytes 8388608 | tf_op jit(solution)/shard_map/pallas_call | solution.py:336
  97.3 2.9 %shard_map.51 = (bf16[1,1024,512]{2,1,0:T(8,128)(2,1)}, bf16[512,2304]{1,0:T(8,128)(2,1)}) custom-call(bf16[1,1024,512]{2,1,0:T(8,128)(2,1)} %get-tuple-element.4.a_in, bf16[512,2304]{1,0:T(8,128)(2,1)} %get-tuple-element.5.b_in), custom_call_target="tpu_custom_call" | custom-call | bytes 7340032 | tf_op jit(solution)/shard_map/pallas_call | solution.py:366
